TPU v7x, 128 devices: a whole 4x4x4 slice. The times are simulated.
128 devices in a mesh: row: 16 (over y, z_hi, core), col: 8 (over x, z_lo).
Axes of the slice: x: 4, y: 4, z: 4 (z_hi: 2, z_lo: 2; z = z_hi * 2 + z_lo), core: 2. Of those that a mesh axis runs over, the one named last changes fastest.
Arguments:
- activations: bfloat16 [4096, 4096], P(('row', 'col')), may hold values from -6 to 6
- grad_gate: bfloat16 [4096, 14336], P(('row', 'col')), may hold values from -6 to 6
- grad_up: bfloat16 [4096, 14336], P(('row', 'col')), may hold values from -6 to 6
- doc_order: int32 [16], replicated, may hold values from 0 to 15, each once
- seeds: int32 [2], replicated, may hold values from 0 to 1073741823
Outputs:
- sketches: float32 [2, 16, 128], P(None, 'row', 'col')
Inputs may be any that keep to these rules, and one draw needn't show every extreme that they name: `doc_order`: each document appears once.
All inputs are finite; a program needn't handle non-finite values.
Results may differ from a plain program's by a relative error of at most 0.0029.
Values may be sent and summed in bfloat16 or wider, within the bound.
A program may use at most 128 MiB of HBM per device.

v0:
```python
import math

import jax
import jax.numpy as jnp
from jax import lax
from jax.sharding import PartitionSpec as P

D = 4096
FF = 14336
K = 128
SEQ = 256


def hash_mix(value_in):
    value_in = value_in ^ lax.shift_right_logical(value_in, jnp.full_like(value_in, 16))
    value_in = value_in * -2048144789
    value_in = value_in ^ lax.shift_right_logical(value_in, jnp.full_like(value_in, 13))
    value_in = value_in * -1028477387
    value_in = value_in ^ lax.shift_right_logical(value_in, jnp.full_like(value_in, 16))
    return value_in


def sign_planes(row_begin, row_count, col_begin, col_count, row_width, seed_value):
    row_ids = row_begin + jnp.arange(row_count, dtype=jnp.int32)
    col_ids = col_begin + jnp.arange(col_count, dtype=jnp.int32)
    counter = row_ids[:, None] * row_width + col_ids[None, :]
    word_count = K // 32
    word_ids = jnp.arange(word_count, dtype=jnp.int32)
    hashed = hash_mix(
        hash_mix(counter[None, :, :] * word_count + word_ids[:, None, None]) + seed_value
    )
    full_shape = (word_count, 32, row_count, col_count)
    bit_ids = jnp.arange(32, dtype=jnp.int32)[None, :, None, None]
    shifted = lax.shift_right_logical(
        jnp.broadcast_to(hashed[:, None, :, :], full_shape), jnp.broadcast_to(bit_ids, full_shape)
    )
    sign_bits = (shifted & 1).reshape(K, row_count, col_count)
    return jnp.where(sign_bits == 1, -1.0, 1.0).astype(jnp.bfloat16)


def sketch_matrix(grads, tokens_cols, seed_value, row_base, col_base):
    doc_count = tokens_cols.shape[0] // SEQ
    own_rows = grads.shape[1]
    own_cols = tokens_cols.shape[1]
    gradient = jnp.einsum(
        "ntr,ntc->nrc",
        grads.reshape(doc_count, SEQ, own_rows),
        tokens_cols.reshape(doc_count, SEQ, own_cols),
        preferred_element_type=jnp.float32,
    ).astype(jnp.bfloat16)
    row_block = math.gcd(own_rows, max(1, 65536 // own_cols))

    def add_block(block_id, running):
        begin_row = block_id * row_block
        picked = lax.dynamic_slice_in_dim(gradient, begin_row, row_block, 1)
        signs_here = sign_planes(row_base + begin_row, row_block, col_base, own_cols, D, seed_value)
        return running + jnp.einsum(
            "nrc,krc->nk", picked, signs_here, preferred_element_type=jnp.float32
        )

    return lax.fori_loop(
        0, own_rows // row_block, add_block, jnp.zeros((doc_count, K), jnp.float32)
    )


def shards(activations, grad_gate, grad_up, doc_order, seeds):
    row_count = lax.axis_size("row")
    col_count = lax.axis_size("col")
    total_docs = doc_order.shape[0]
    split_cols = lax.all_to_all(activations, "col", split_axis=1, concat_axis=0, tiled=True)
    tokens_cols = lax.all_gather(split_cols, "row", axis=0, tiled=True)
    wide_gate, wide_up = (
        lax.all_gather(grad_gate, "col", axis=0, tiled=True),
        lax.all_gather(grad_up, "col", axis=0, tiled=True),
    )
    gate_rows, up_rows = (
        lax.all_to_all(wide_gate, "row", split_axis=1, concat_axis=0, tiled=True),
        lax.all_to_all(wide_up, "row", split_axis=1, concat_axis=0, tiled=True),
    )
    row_base = lax.axis_index("row") * gate_rows.shape[1]
    col_base = lax.axis_index("col") * tokens_cols.shape[1]
    gate_part = sketch_matrix(gate_rows, tokens_cols, seeds[0], row_base, col_base)
    up_part = sketch_matrix(up_rows, tokens_cols, seeds[1], row_base, col_base)
    partial_sums = jnp.stack([gate_part, up_part])
    onehot = (doc_order[None, :] == jnp.arange(total_docs, dtype=jnp.int32)[:, None]).astype(
        jnp.float32
    )
    placed = jnp.einsum("dn,mnk->mdk", onehot, partial_sums, precision=lax.Precision.HIGHEST)
    scale = 1.0 / math.sqrt(SEQ * D * FF)
    total = lax.psum(placed, ("row", "col"))
    docs_here = total_docs // row_count
    coords_here = K // col_count
    mine = lax.dynamic_slice(
        total,
        (jnp.int32(0), lax.axis_index("row") * docs_here, lax.axis_index("col") * coords_here),
        (2, docs_here, coords_here),
    )
    return mine * scale


def solution(mesh):
    in_specs = (P(("row", "col"), None), P(("row", "col"), None), P(("row", "col"), None), P(), P())
    out_specs = P(None, "row", "col")
    return jax.shard_map(shards, mesh=mesh, in_specs=in_specs, out_specs=out_specs, check_vma=False)
```

profile of v0, /device:TPU:1, one launch (start us, length us, event | category | flops | bytes accessed | tf_op | source)
XLA Modules:
  0.0 981.1 jit_solution(4781454951784406652)
XLA Ops:
  9.0 12.0 %all_to_all.51 = bf16[32,8,512]{2,0,1:T(8,128)(2,1)} all-to-all(bf16[32,8,512]{2,0,1:T(8,128)(2,1)S(1)} %bitcast.76), channel_id=1, replica_groups=mesh['row'=16,'col'=8] {'col'}, dimensions={1} | all-to-all | bytes 524288 | tf_op jit(solution)/shard_map/all_to_all | solution.py:70
  21.1 139.9 %all-gather.4.cloned.1.call-done = bf16[256,14336]{1,0:T(8,128)(2,1)} async-done(((bf16[32,14336]{1,0:T(8,128)(2,1)}), bf16[256,14336]{1,0:T(8,128)(2,1)}) %all-gather.4.cloned.1.call-update) | async-done | bytes 7340048 | tf_op jit(solution)/shard_map/all_gather | solution.py:73
  161.0 10.4 %copy.22 = bf16[256,14336]{0,1:T(8,128)(2,1)} copy(bf16[256,14336]{1,0:T(8,128)(2,1)} %all-gather.4.cloned.1.call-done) | data formatting | bytes 14680064 | tf_op jit(solution)/shard_map/all_gather | solution.py:73
  171.4 7.7 all-to-all-start
  179.7 213.1 %all-gather.8.cloned.1.call-done = bf16[256,14336]{1,0:T(8,128)(2,1)} async-done(((bf16[32,14336]{1,0:T(8,128)(2,1)}), bf16[256,14336]{1,0:T(8,128)(2,1)}) %all-gather.8.cloned.1.call-update) | async-done | bytes 7340048 | tf_op jit(solution)/shard_map/all_gather | solution.py:74
  392.8 10.1 %copy.25 = bf16[256,14336]{0,1:T(8,128)(2,1)} copy(bf16[256,14336]{1,0:T(8,128)(2,1)} %all-gather.8.cloned.1.call-done) | data formatting | bytes 14680064 | tf_op jit(solution)/shard_map/all_gather | solution.py:74
  402.9 7.3 all-to-all-start.2
  410.2 111.2 %all-gather.6.cloned.1.call-done = bf16[4096,512]{1,0:T(8,128)(2,1)} async-done(((bf16[256,512]{1,0:T(8,128)(2,1)}), bf16[4096,512]{1,0:T(8,128)(2,1)}) %all-gather.6.cloned.1.call-update) | async-done | bytes 4194320 | tf_op jit(solution)/shard_map/all_gather | solution.py:71
  521.4 10.5 %convolution_convert_fusion.1 = bf16[16,896,512]{2,1,0:T(8,128)(2,1)} fusion(bf16[16,256,512]{2,1,0:T(8,128)(2,1)} %bitcast.71, bf16[256,16,896]{0,2,1:T(8,128)(2,1)} %all-to-all-done), kind=kOutput, calls=%fused_computation.43 | convolution fusion | flops 3765436416 | bytes 26214400 | tf_op jit(solution)/shard_map/ntr,ntc->nrc/dot_general | solution.py:45
  531.9 183.2 %while.28 = (s32[]{:T(128)}, f32[16,128]{1,0:T(8,128)S(1)}, bf16[16,896,512]{2,1,0:T(8,128)(2,1)}, s32[]{:T(128)}, s32[]{:T(128)}, /*index=5*/s32[]{:T(128)}, s32[]{:T(128)}, s32[]{:T(128)}, s32[]{:T(128)}, s32[]{:T(128)}) while((s32[]{:T(128)}, f32[16,128]{1,0:T(8,128)S(1)}, bf16[16,896,512]{2,1,0:T(8,128)(2,1)}, s32[]{:T(128)}, ...), condition=%wide.region_1.2_spmd.clone, body=%wide.region_0.1_spmd.clone.sunk | while | flops 315233024 | bytes 48782520 | solution.py:61
  535.0 3.4 copy.36
  542.5 7.5 select_convert_fusion.4
  550.0 8.1 fusion.40
  558.0 3.1 constant_dynamic-slice_fusion.4
  561.2 3.4 copy.36
  568.6 7.5 select_convert_fusion.4
  576.1 8.1 fusion.40
  584.2 3.1 constant_dynamic-slice_fusion.4
  587.3 3.4 copy.36
  594.8 7.5 select_convert_fusion.4
  602.3 8.1 fusion.40
  610.4 3.1 constant_dynamic-slice_fusion.4
  613.5 3.4 copy.36
  621.0 7.5 select_convert_fusion.4
  628.5 8.1 fusion.40
  636.6 3.1 constant_dynamic-slice_fusion.4
  639.7 3.4 copy.36
  647.2 7.5 select_convert_fusion.4
  654.7 8.1 fusion.40
  662.8 3.1 constant_dynamic-slice_fusion.4
  665.9 3.4 copy.36
  673.4 7.5 select_convert_fusion.4
  680.9 8.1 fusion.40
  689.0 3.1 constant_dynamic-slice_fusion.4
  692.1 3.4 copy.36
  699.6 7.5 select_convert_fusion.4
  707.0 8.1 fusion.40
  715.1 10.5 %convolution_convert_fusion = bf16[16,896,512]{2,1,0:T(8,128)(2,1)} fusion(bf16[16,256,512]{2,1,0:T(8,128)(2,1)} %bitcast.72, bf16[256,16,896]{0,2,1:T(8,128)(2,1)} %all-to-all-done.2), kind=kOutput, calls=%fused_computation.42 | convolution fusion | flops 3765436416 | bytes 26214400 | tf_op jit(solution)/shard_map/ntr,ntc->nrc/dot_general | solution.py:45
  725.7 183.7 %while.29 = (s32[]{:T(128)}, f32[16,128]{1,0:T(8,128)S(1)}, bf16[16,896,512]{2,1,0:T(8,128)(2,1)}, s32[]{:T(128)}, s32[]{:T(128)}, /*index=5*/s32[]{:T(128)}, s32[]{:T(128)}, s32[]{:T(128)}, s32[]{:T(128)}, s32[]{:T(128)}) while((s32[]{:T(128)}, f32[16,128]{1,0:T(8,128)S(1)}, bf16[16,896,512]{2,1,0:T(8,128)(2,1)}, s32[]{:T(128)}, ...), condition=%wide.region_3.4_spmd.clone, body=%wide.region_2.3_spmd.clone.sunk | while | flops 315233024 | bytes 48782520 | solution.py:61
  725.7 3.1 constant_dynamic-slice_fusion.5
  728.8 3.4 copy.38
  736.3 7.5 select_convert_fusion.5
  743.8 8.1 fusion.43
  751.9 3.1 constant_dynamic-slice_fusion.5
  755.0 3.4 copy.38
  762.6 7.5 select_convert_fusion.5
  770.1 8.1 fusion.43
  778.2 3.1 constant_dynamic-slice_fusion.5
  781.3 3.4 copy.38
  788.8 7.5 select_convert_fusion.5
  796.3 8.1 fusion.43
  807.5 3.4 copy.38
  815.1 7.5 select_convert_fusion.5
  822.6 8.1 fusion.43
  833.8 3.4 copy.38
  841.3 7.5 select_convert_fusion.5
  848.8 8.1 fusion.43
  860.0 3.4 copy.38
  867.6 7.5 select_convert_fusion.5
  875.1 8.1 fusion.43
  886.3 3.4 copy.38
  893.8 7.5 select_convert_fusion.5
  901.3 8.1 fusion.43
  909.5 64.4 %psum.7 = f32[2,16,128]{2,1,0:T(8,128)S(1)} all-reduce(f32[2,16,128]{2,1,0:T(8,128)S(1)} %convolution_bitcast_fusion.2), channel_id=1, replica_groups=mesh['row'=16,'col'=8] {'row','col'}, use_global_device_ids=true, to_apply=%region_4.5 | all-reduce | flops 4096 | bytes 32768 | tf_op jit(solution)/shard_map/psum | solution.py:90
  (121 shorter events, 75.9 us)
Async XLA Ops:
  6.5 154.4 %all-gather.4.cloned.1.call-start = ((), (), s32[]{:S(2)}) async-start(), calls=%async_computation.3 | async-start | bytes 8257536 | tf_op jit(solution)/shard_map/all_gather | solution.py:73
  7.3 385.5 %all-gather.8.cloned.1.call-start = ((), (), s32[]{:S(2)}) async-start(), calls=%async_computation.5 | async-start | bytes 8257536 | tf_op jit(solution)/shard_map/all_gather | solution.py:74
  8.0 513.4 %all-gather.6.cloned.1.call-start = ((), (), s32[]{:S(2)}) async-start(), calls=%async_computation.4 | async-start | bytes 4456448 | tf_op jit(solution)/shard_map/all_gather | solution.py:71
  21.1 158.0 %copy-start = (s32[2]{0:T(128)S(1)}, s32[2]{0:T(128)}, u32[]{:S(2)}) copy-start(s32[2]{0:T(128)} %param.13) | copy-start | bytes 28
  171.4 231.5 %all-to-all-start = ((bf16[256,16,896]{0,2,1:T(8,128)(2,1)}), bf16[256,16,896]{0,2,1:T(8,128)(2,1)}, u32[]{:S(2)}, u32[]{:S(2)}) async-start(bf16[256,16,896]{0,2,1:T(8,128)(2,1)} %bitcast.74), calls=%async_computation | async-start | bytes 14680064 | tf_op jit(solution)/shard_map/all_to_all | solution.py:77
  402.9 312.2 %all-to-all-start.2 = ((bf16[256,16,896]{0,2,1:T(8,128)(2,1)}), bf16[256,16,896]{0,2,1:T(8,128)(2,1)}, u32[]{:S(2)}, u32[]{:S(2)}) async-start(bf16[256,16,896]{0,2,1:T(8,128)(2,1)} %bitcast.73), calls=%async_computation.2 | async-start | bytes 14680064 | tf_op jit(solution)/shard_map/all_to_all | solution.py:78
  725.7 183.8 %copy-start.1 = (s32[16]{0:T(128)S(1)}, s32[16]{0:T(128)}, u32[]{:S(2)}) copy-start(s32[16]{0:T(128)} %param.12) | copy-start | bytes 196
Sparse Core Ops, SparseCore 0:
  9.0 151.9 all-gather.3
  162.6 230.1 all-gather.7
  395.2 126.1 all-gather.5
where the time goes:
time: 984 us; the launch traced here: 981 us
  waiting for transfers between devices  466 us (47%)
  local copies, waits for them, and re-layouts  138 us (14%)
  other arithmetic  138 us (14%)
  matrix products  134 us (14%)
  blocking collectives  76.5 us (8%)
  starting transfers between devices  15 us (2%)
  between operations  13.2 us (1%)
    all_gather x1, waiting for transfers between devices, shards(): lax.all_gather(grad_up, 'col', axis=0, tiled=True)  213 us
    all_gather x1, waiting for transfers between devices, shards(): lax.all_gather(grad_gate, 'col', axis=0, tiled=True)  140 us
    dot_general x14, matrix products, add_block(): jnp.einsum('nrc,krc->nk', picked, signs_here, preferred_element_type=jnp....  113 us
    all_gather x1, waiting for transfers between devices, shards(): tokens_cols = lax.all_gather(split_cols, 'row', axis=0, tiled=True)  111 us
    convert_element_type x14, other arithmetic, sign_planes(): return jnp.where(sign_bits == 1, -1.0, 1.0).astype(jnp.bfloat16)  105 us
    dynamic_slice x28, local copies, waits for them, and re-layouts, add_block(): picked = lax.dynamic_slice_in_dim(gradient, begin_row, row_block, 1)  91.8 us
    psum x1, blocking collectives, shards(): total = lax.psum(placed, ('row', 'col'))  64.4 us
    xor x14, other arithmetic, hash_mix(): value_in ^ lax.shift_right_logical(value_in, jnp.full_like(value_in, 16))  31.4 us
  transfers between devices with their start and end apart: 5, of which 3 were waited for; matrix products, arithmetic and copies ran while one was open for 22% of the time, Pallas kernels for 0%

commit v1 on v0

v1 whole, which is shorter than its diff:
```python
import functools
import math

import jax
import jax.numpy as jnp
from jax import lax
from jax.experimental import pallas as pl
from jax.experimental.pallas import tpu as pltpu
from jax.sharding import PartitionSpec as P

D = 4096
FF = 14336
K = 128
SEQ = 256
MESH = pl.DeviceIdType.MESH
BF16 = jnp.bfloat16
ROWS = 896
COLS = 1024
CH = 128
NQ = ROWS // CH
NP = 2
PW = COLS // NP


def lsr(value, count):
    return lax.shift_right_logical(value, jnp.full_like(value, count))


def hash_mix(v):
    v = v ^ lsr(v, 16)
    v = v * -2048144789
    v = v ^ lsr(v, 13)
    v = v * -1028477387
    return v ^ lsr(v, 16)


def device_of(x, y, z, k):
    return (y * 4 + (z // 2) * 2 + k, x * 2 + lax.rem(z, 2))


def kernel(
    act_in, gate_in, up_in, order_ref, seed_ref, out_ref,
    acts, grads, words, gs, acc, part, fin1, mid, fin2,
    r_s0, r_s1, r_s2, r_s3, r_a2a, r_ring, r_f1, r_f2,
    s_s0, s_s1, s_s2, s_s3, s_a2a, s_ring, s_f1, s_f2,
):
    row = lax.axis_index("row")
    col = lax.axis_index("col")
    y = row // 4
    zh = lax.rem(row // 2, 2)
    k = lax.rem(row, 2)
    x = col // 2
    zl = lax.rem(col, 2)
    z = zh * 2 + zl
    me = (y * 4 + z) * 2 + k

    def at_x(dx):
        return device_of(lax.rem(x + dx, 4), y, z, k)

    def at_y(dy):
        return device_of(x, lax.rem(y + dy, 4), z, k)

    def at_z(dz):
        return device_of(x, y, lax.rem(z + dz, 4), k)

    sibling = device_of(x, y, z, 1 - k)

    barrier = pltpu.get_barrier_semaphore()

    def greet(j, _):
        t = lax.rem(me + j, 32)
        pl.semaphore_signal(
            barrier, inc=1, device_id=device_of(x, t // 8, lax.rem(t // 2, 4), lax.rem(t, 2)), device_id_type=MESH
        )
        return 0

    lax.fori_loop(1, 32, greet, 0)
    for dx in range(1, 4):
        for dz in range(2):
            pl.semaphore_signal(
                barrier, inc=1,
                device_id=(row, lax.rem(x + dx, 4) * 2 + lax.rem(zl + dz, 2)), device_id_type=MESH,
            )
    pl.semaphore_wait(barrier, 37)

    def remote(src, dst, send, recv, target):
        return pltpu.make_async_remote_copy(
            src_ref=src, dst_ref=dst, send_sem=send, recv_sem=recv, device_id=target, device_id_type=MESH
        )

    def arrive(ref, sem):
        pltpu.make_async_copy(ref, ref, sem).wait()

    def act_slice(c):
        return lambda p: act_in.at[:, pl.ds(pl.multiple_of(c * COLS + p * PW, PW), PW)]

    def s0(p):
        own = acts.at[p, k, zh, y, x, zl]
        pltpu.make_async_copy(act_slice(x)(p), own, r_s0.at[p]).start()
        for dx in range(1, 4):
            c = lax.rem(x + dx, 4)
            remote(act_slice(c)(p), own, s_s0.at[p, dx - 1], r_s0.at[p], at_x(dx)).start()

    def s0_done(p):
        for dx in range(1, 4):
            own = acts.at[p, k, zh, y, x, zl]
            remote(act_slice(lax.rem(x + dx, 4))(p), own, s_s0.at[p, dx - 1], r_s0.at[p], at_x(dx)).wait_send()

    def s1_copy(p, i, target):
        block = acts.at[p, k, zh, y, :, zl]
        return remote(block, block, s_s1.at[p, i - 1], r_s1.at[p], target)

    def s1(p):
        arrive(acts.at[p, 0, 0, 0, :, 0], r_s0.at[p])

        @pl.when(k == 0)
        def _():
            for i in range(1, 4):
                s1_copy(p, i, at_y(i)).start()

        @pl.when(k == 1)
        def _():
            for i in range(1, 4):
                s1_copy(p, i, at_z(i)).start()

    def line(p, core, step, half=None):
        if core == 0:
            zz = lax.rem(z + step, 4)
            ys = pl.ds(0, 4) if half is None else pl.ds(half * 2, 2)
            return acts.at[p, 0, zz // 2, ys, :, lax.rem(zz, 2)]
        yy = lax.rem(y + step, 4)
        if half is None:
            return acts.at[p, 1, :, yy]
        return acts.at[p, 1, half, yy]

    def nxt(core, step):
        return at_z(step) if core == 0 else at_y(step)

    def s2_copy(p, core, which):
        ref = [line(p, core, 0), line(p, core, 0), line(p, core, 3, 0), line(p, core, 1, 1)][which]
        return remote(ref, ref, s_s2.at[p, which], r_s2.at[p, which], nxt(core, 1 if which % 2 == 0 else 3))

    def s3_copy(p, core, which):
        ref = [
            line(p, core, 0), line(p, core, 3), line(p, core, 1), line(p, core, 2, 0), line(p, core, 2, 1)
        ][which]
        return remote(ref, ref, s_s3.at[p, which], r_s3.at[p], sibling)

    def by_core(f):
        @pl.when(k == 0)
        def _():
            f(0)

        @pl.when(k == 1)
        def _():
            f(1)

    full = lambda p: acts.at[p, 0, 0, :, :, 0]
    half = lambda p: acts.at[p, 0, 0, pl.ds(0, 2), :, 0]

    def s2(p):
        arrive(acts.at[p, 0, 0, pl.ds(0, 3), :, 0], r_s1.at[p])

        def go(core):
            s2_copy(p, core, 0).start()
            s2_copy(p, core, 1).start()
            s3_copy(p, core, 0).start()

        by_core(go)

    def s2_on(p):
        arrive(full(p), r_s2.at[p, 0])

        def go_left(core):
            s2_copy(p, core, 2).start()
            s3_copy(p, core, 1).start()

        by_core(go_left)
        arrive(full(p), r_s2.at[p, 1])

        def go_right(core):
            s2_copy(p, core, 3).start()
            s3_copy(p, core, 2).start()

        by_core(go_right)

    def s3(p):
        arrive(half(p), r_s2.at[p, 2])
        by_core(lambda core: s3_copy(p, core, 3).start())
        arrive(half(p), r_s2.at[p, 3])
        by_core(lambda core: s3_copy(p, core, 4).start())

    def act_ready(p):
        arrive(acts.at[p, 0], r_s3.at[p])

    def act_done(p):
        s0_done(p)

        def go(core):
            for i in range(1, 4):
                s1_copy(p, i, at_y(i) if core == 0 else at_z(i)).wait_send()
            for w in range(4):
                s2_copy(p, core, w).wait_send()
            for w in range(5):
                s3_copy(p, core, w).wait_send()

        by_core(go)

    def a2a(q):
        dst = grads.at[q, k, zh, y, x, zl]

        def send(j, _):
            t = lax.rem(me // 2 + j, 16)
            begin = pl.multiple_of(t * ROWS + q * CH, CH)
            ty = t // 4
            tz = lax.rem(t, 4)

            @pl.when((j > 0) | (k == 1))
            def _():
                remote(
                    gate_in.at[:, pl.ds(begin, CH)], dst, s_a2a.at[q], r_a2a.at[q], device_of(x, ty, tz, 0)
                ).start()

            @pl.when((j > 0) | (k == 0))
            def _():
                remote(
                    up_in.at[:, pl.ds(begin, CH)], dst, s_a2a.at[q], r_a2a.at[q], device_of(x, ty, tz, 1)
                ).start()

            return 0

        begin = pl.multiple_of((me // 2) * ROWS + q * CH, CH)

        @pl.when(k == 0)
        def _():
            pltpu.make_async_copy(gate_in.at[:, pl.ds(begin, CH)], dst, r_a2a.at[q]).start()

        @pl.when(k == 1)
        def _():
            pltpu.make_async_copy(up_in.at[:, pl.ds(begin, CH)], dst, r_a2a.at[q]).start()

        lax.fori_loop(0, 16, send, 0)

    def ring_copy(q, which):
        at = [0, 0, 3, 1][which]
        xx = lax.rem(x + at, 4)
        ref = grads.at[q, :, :, :, xx] if which < 2 else grads.at[q, which - 2, :, :, xx]
        return remote(ref, ref, s_ring.at[q, which], r_ring.at[q, which], at_x(1 if which % 2 == 0 else 3))

    def ring(q):
        arrive(grads.at[q, :, :, :, 0], r_a2a.at[q])
        ring_copy(q, 0).start()
        ring_copy(q, 1).start()

    def ring_on(q):
        arrive(grads.at[q, :, :, :, 0], r_ring.at[q, 0])
        ring_copy(q, 2).start()
        arrive(grads.at[q, :, :, :, 0], r_ring.at[q, 1])
        ring_copy(q, 3).start()

    def grad_ready(q):
        arrive(grads.at[q, 0, :, :, 0], r_ring.at[q, 2])
        arrive(grads.at[q, 0, :, :, 0], r_ring.at[q, 3])

    def grad_done(q, _):
        sent = gate_in.at[:, pl.ds(0, 31 * CH)]
        pltpu.make_async_copy(sent, sent, s_a2a.at[q]).wait()
        for w in range(4):
            ring_copy(q, w).wait_send()
        return 0

    seed = jnp.where(k == 0, seed_ref[0], seed_ref[1])
    row_base = (y * 4 + z) * ROWS
    col_base = x * COLS

    def hash_chunk(q):
        it = lax.broadcasted_iota(jnp.int32, (8, COLS), 0)
        jt = lax.broadcasted_iota(jnp.int32, (8, COLS), 1)
        base = ((row_base + lsr(it, 2)) * D + col_base + jt) * 4 + (it & 3)

        def two_rows(t, _):
            for u in range(2):
                tt = q * (CH // 2) + t * 2 + u
                h = hash_mix(hash_mix(base + tt * (2 * D * 4)) + seed)
                words[tt] = jnp.concatenate([h, lsr(h, 16)], 0).astype(jnp.int16)
            return 0

        lax.fori_loop(0, CH // 4, two_rows, 0)

    pair_of = lsr(lax.broadcasted_iota(jnp.int32, (256, 256), 1) & 15, 1)

    def work(q, p_lo, p_hi):
        def eight_docs(d, _):
            for c in range(2):
                for yy in range(4):
                    gt = grads[q, d, c, yy].reshape(SEQ, CH).T
                    for p in range(p_lo, p_hi):
                        a = acts[p, d, c, yy].reshape(SEQ, PW)
                        g = jnp.dot(gt, a, preferred_element_type=jnp.float32)
                        gs[d * 8 + c * 4 + yy, :, p * PW:(p + 1) * PW] = g.astype(BF16)
            return 0

        lax.fori_loop(0, 2, eight_docs, 0)
        lo, hi = p_lo * PW, p_hi * PW

        def rows_32(t, _):
            for v in range(2):
                begin = pl.multiple_of(t * 32 + v * 16, 16)
                g = jnp.concatenate([gs[n, pl.ds(begin, 16), lo:hi] for n in range(16)], 0)
                picked = None
                for pair in range(8):
                    w = words[q * (CH // 2) + t * 16 + v * 8 + pair, :, lo:hi]
                    s = jnp.concatenate(
                        [
                            jnp.where(
                                (w & jnp.int16((1 << b) if b < 15 else -32768)) != 0, BF16(-1.0), BF16(1.0)
                            )
                            for b in range(16)
                        ],
                        0,
                    )
                    r = lax.dot_general(s, g, (((1,), (1,)), ((), ())), preferred_element_type=jnp.float32)
                    picked = r if picked is None else jnp.where(pair_of == pair, r, picked)
                acc[...] += picked
            return 0

        lax.fori_loop(0, CH // 32, rows_32, 0)

    acc[...] = jnp.zeros_like(acc)
    s0(0)
    a2a(0)
    s0(1)
    s1(0)
    s1(1)
    a2a(1)
    hash_chunk(0)
    s2(0)
    ring(0)
    s2(1)
    hash_chunk(1)
    hash_chunk(2)
    s2_on(0)
    ring(1)
    hash_chunk(3)
    s3(0)
    ring_on(0)
    s2_on(1)
    a2a(2)
    hash_chunk(4)
    a2a(3)
    s3(1)
    act_ready(0)
    grad_ready(0)
    ring_on(1)
    work(0, 0, 1)
    a2a(4)
    ring(2)
    grad_ready(1)
    work(1, 0, 1)
    act_ready(1)
    a2a(5)
    a2a(6)
    work(0, 1, 2)
    ring_on(2)
    ring(3)
    work(1, 1, 2)
    hash_chunk(5)
    hash_chunk(6)

    def chunk(q, _):
        grad_ready(q)

        @pl.when(q + 1 < NQ)
        def _():
            ring_on(q + 1)

        @pl.when(q + 2 < NQ)
        def _():
            ring(q + 2)

        work(q, 0, 2)
        return 0

    lax.fori_loop(2, NQ, chunk, 0)

    ri = lax.broadcasted_iota(jnp.int32, (256, 256), 0)
    ci = lax.broadcasted_iota(jnp.int32, (256, 256), 1)
    kept = jnp.where((lsr(ri, 2) & 1) == (ci & 1), acc[...], 0.0)
    cf = lsr(lax.broadcasted_iota(jnp.int32, (256, 16), 0), 4)
    df = lax.broadcasted_iota(jnp.int32, (256, 16), 1)
    fold = jnp.zeros((256, 16), jnp.float32)
    for n in range(16):
        doc = order_ref[(n % 4) * 4 + ((n // 4) % 2) * 2 + n // 8]
        fold = jnp.where((cf == n) & (df == doc), 1.0, fold)
    rk = lax.broadcasted_iota(jnp.int32, (256, 128), 0)
    ck = lax.broadcasted_iota(jnp.int32, (256, 128), 1)
    place = jnp.where((rk & 3) * 32 + (lsr(rk, 3) & 1) * 16 + lsr(rk, 4) == ck, 1.0, 0.0)
    by_doc = jnp.dot(kept, fold, precision=lax.Precision.HIGHEST, preferred_element_type=jnp.float32)
    mine = lax.dot_general(
        by_doc, place, (((0,), (0,)), ((), ())),
        precision=lax.Precision.HIGHEST, preferred_element_type=jnp.float32,
    )
    for d in range(16):
        part[d] = jnp.broadcast_to(mine[d:d + 1, :], (8, 128))

    def f1_copy(j):
        t = lax.rem(row + j, 16)
        return remote(part.at[t], fin1.at[row], s_f1, r_f1, (t, col))

    pltpu.make_async_copy(part.at[row], fin1.at[row], r_f1).start()
    lax.fori_loop(1, 16, lambda j, _: (f1_copy(j).start(), 0)[1], 0)
    arrive(fin1, r_f1)
    for m in range(2):
        total = fin1[m]
        for r in range(1, 8):
            total = total + fin1[r * 2 + m]
        mid[m] = total

    def f2_copy(j):
        return remote(mid, fin2.at[col], s_f2.at[j - 1], r_f2, (row, lax.rem(col + j, 8)))

    pltpu.make_async_copy(mid, fin2.at[col], r_f2).start()
    for j in range(1, 8):
        f2_copy(j).start()
    arrive(fin2, r_f2)
    total = fin2[0]
    for c in range(1, 8):
        total = total + fin2[c]
    out_ref[...] = total * (1.0 / math.sqrt(SEQ * D * FF))

    for p in range(NP):
        act_done(p)
    lax.fori_loop(0, NQ, grad_done, 0)
    sent = part.at[pl.ds(0, 15)]
    pltpu.make_async_copy(sent, sent, s_f1).wait()
    for j in range(1, 8):
        f2_copy(j).wait_send()


def shards(activations, grad_gate, grad_up, doc_order, seeds):
    dma = pltpu.SemaphoreType.DMA
    total = pl.pallas_call(
        kernel,
        out_shape=jax.ShapeDtypeStruct((2, 8, K), jnp.float32),
        in_specs=[pl.BlockSpec(memory_space=pl.ANY)] * 3 + [pl.BlockSpec(memory_space=pltpu.SMEM)] * 2,
        out_specs=pl.BlockSpec(memory_space=pltpu.VMEM),
        scratch_shapes=[
            pltpu.VMEM((NP, 2, 2, 4, 4, 2, 32, PW), BF16),
            pltpu.VMEM((NQ, 2, 2, 4, 4, 2, 32, CH), BF16),
            pltpu.VMEM((ROWS // 2, 16, COLS), jnp.int16),
            pltpu.VMEM((16, CH, COLS), BF16),
            pltpu.VMEM((256, 256), jnp.float32),
            pltpu.VMEM((16, 8, K), jnp.float32),
            pltpu.VMEM((16, 8, K), jnp.float32),
            pltpu.VMEM((2, 8, K), jnp.float32),
            pltpu.VMEM((8, 2, 8, K), jnp.float32),
            dma((NP,)), dma((NP,)), dma((NP, 4)), dma((NP,)), dma((NQ,)), dma((NQ, 4)), dma, dma,
            dma((NP, 3)), dma((NP, 3)), dma((NP, 4)), dma((NP, 5)), dma((NQ,)), dma((NQ, 4)), dma, dma((7,)),
        ],
        compiler_params=pltpu.CompilerParams(
            collective_id=0, has_side_effects=True, vmem_limit_bytes=56 * 2**20
        ),
        name="sketch",
    )(activations, grad_gate, grad_up, doc_order, seeds)
    col = lax.axis_index("col")
    return lax.dynamic_slice(total, (jnp.int32(0), jnp.int32(0), col * 16), (2, 1, 16))


def solution(mesh):
    in_specs = (P(("row", "col"), None), P(("row", "col"), None), P(("row", "col"), None), P(), P())
    out_specs = P(None, "row", "col")
    return jax.shard_map(shards, mesh=mesh, in_specs=in_specs, out_specs=out_specs, check_vma=False)
```

time: 984 us -> 147 us (0.15)
  waiting for transfers between devices: 466 us -> 0 us
  Pallas kernels: 0 us -> 146 us
  other arithmetic: 138 us -> 0 us
  local copies, waits for them, and re-layouts: 138 us -> 1.34 us
  matrix products: 134 us -> 0 us
  blocking collectives: 76.5 us -> 0 us
  starting transfers between devices: 15 us -> 0 us
  between operations: 13.2 us -> 0.01 us
    all_gather x3 -> x0, waiting for transfers between devices: 464 us -> none  [the longest x1 213 us: shards(): lax.all_gather(grad_up, 'col', axis=0, tiled=True)]
    pallas_call x0 -> x1, Pallas kernels: none -> 146 us  [shards(): pl.pallas_call(kernel, out_shape=jax.ShapeDtypeStruct((2, 8, K), jnp.floa...]
    dot_general x17 -> x0, matrix products: 134 us -> none  [the longest x14 113 us: add_block(): jnp.einsum('nrc,krc->nk', picked, signs_here, preferred_element_type=jnp....]
    convert_element_type x14 -> x0, other arithmetic: 105 us -> none  [sign_planes(): return jnp.where(sign_bits == 1, -1.0, 1.0).astype(jnp.bfloat16)]
    dynamic_slice x28 -> x1, local copies, waits for them, and re-layouts: 91.8 us -> 1.34 us  [shards(): lax.dynamic_slice(total, (jnp.int32(0), jnp.int32(0), col * 16), (2, 1, 16))]
    psum x1 -> x0, blocking collectives: 64.4 us -> none  [shards(): total = lax.psum(placed, ('row', 'col'))]
    xor x14 -> x0, other arithmetic: 31.4 us -> none  [hash_mix(): value_in ^ lax.shift_right_logical(value_in, jnp.full_like(value_in, 16))]
    xor x14 -> x0, local copies, waits for them, and re-layouts: 22.5 us -> none  [hash_mix(): value_in ^ lax.shift_right_logical(value_in, jnp.full_like(value_in, 16))]
  transfers between devices with their start and end apart: 5 -> 0, of which waited for: 3 -> 0; matrix products, arithmetic and copies ran while one was open for 22% -> 0% of each run, Pallas kernels for 0% -> 0%
where the time goes in v1:
time: 147 us
  Pallas kernels  146 us (99%)
    pallas_call x1, Pallas kernels, shards(): pl.pallas_call(kernel, out_shape=jax.ShapeDtypeStruct((2, 8, K), jnp.floa...  146 us

profile of v1, /device:TPU:1, one launch (start us, length us, event | category | flops | bytes accessed | tf_op | source)
XLA Modules:
  0.0 146.9 jit_solution(12844364549050258072)
XLA Ops:
  0.0 145.5 %sketch.1 = f32[2,8,128]{2,1,0:T(8,128)} custom-call(bf16[32,4096]{1,0:T(8,128)(2,1)} %act_in.1, bf16[32,14336]{1,0:T(8,128)(2,1)} %gate_in.1, bf16[32,14336]{1,0:T(8,128)(2,1)} %up_in.1, s32[16]{0:T(128)} %order_ref.1, s32[2]{0:T(128)} %seed_ref.1), custom_call_target="tpu_custom_call" | custom-call | tf_op jit(solution)/shard_map/sketch/pallas_call | solution.py:442
  145.6 1.3 constant_dynamic-slice_fusion

commit v2 on v1

--- a/solution.py
+++ b/solution.py
@@ -18,8 +18,9 @@
 COLS = 1024
 CH = 128
 NQ = ROWS // CH
-NP = 2
-PW = COLS // NP
+PIECE = (256, 256, 512)
+BEGIN = (0, 256, 512)
+NP = 3
 
 
 def lsr(value, count):
@@ -40,10 +41,11 @@
 
 def kernel(
     act_in, gate_in, up_in, order_ref, seed_ref, out_ref,
-    acts, grads, words, gs, acc, part, fin1, mid, fin2,
+    acts0, acts1, acts2, grads, words, gs, acc, part, fin1, mid, fin2,
     r_s0, r_s1, r_s2, r_s3, r_a2a, r_ring, r_f1, r_f2,
     s_s0, s_s1, s_s2, s_s3, s_a2a, s_ring, s_f1, s_f2,
 ):
+    acts = (acts0, acts1, acts2)
     row = lax.axis_index("row")
     col = lax.axis_index("col")
     y = row // 4
@@ -81,6 +83,26 @@
                 barrier, inc=1,
                 device_id=(row, lax.rem(x + dx, 4) * 2 + lax.rem(zl + dz, 2)), device_id_type=MESH,
             )
+    seed = jnp.where(k == 0, seed_ref[0], seed_ref[1])
+    row_base = (y * 4 + z) * ROWS
+    col_base = x * COLS
+
+    def hash_chunk(q):
+        it = lax.broadcasted_iota(jnp.int32, (8, COLS), 0)
+        jt = lax.broadcasted_iota(jnp.int32, (8, COLS), 1)
+        base = ((row_base + lsr(it, 2)) * D + col_base + jt) * 4 + (it & 3)
+
+        def two_rows(t, _):
+            for u in range(2):
+                tt = q * (CH // 2) + t * 2 + u
+                h = hash_mix(hash_mix(base + tt * (2 * D * 4)) + seed)
+                words[tt] = jnp.concatenate([h, lsr(h, 16)], 0).astype(jnp.int16)
+            return 0
+
+        lax.fori_loop(0, CH // 4, two_rows, 0)
+
+    hash_chunk(0)
+    hash_chunk(1)
     pl.semaphore_wait(barrier, 37)
 
     def remote(src, dst, send, recv, target):
@@ -92,10 +114,10 @@
         pltpu.make_async_copy(ref, ref, sem).wait()
 
     def act_slice(c):
-        return lambda p: act_in.at[:, pl.ds(pl.multiple_of(c * COLS + p * PW, PW), PW)]
+        return lambda p: act_in.at[:, pl.ds(pl.multiple_of(c * COLS + BEGIN[p], 256), PIECE[p])]
 
     def s0(p):
-        own = acts.at[p, k, zh, y, x, zl]
+        own = acts[p].at[k, zh, y, x, zl]
         pltpu.make_async_copy(act_slice(x)(p), own, r_s0.at[p]).start()
         for dx in range(1, 4):
             c = lax.rem(x + dx, 4)
@@ -103,15 +125,15 @@
 
     def s0_done(p):
         for dx in range(1, 4):
-            own = acts.at[p, k, zh, y, x, zl]
+            own = acts[p].at[k, zh, y, x, zl]
             remote(act_slice(lax.rem(x + dx, 4))(p), own, s_s0.at[p, dx - 1], r_s0.at[p], at_x(dx)).wait_send()
 
     def s1_copy(p, i, target):
-        block = acts.at[p, k, zh, y, :, zl]
+        block = acts[p].at[k, zh, y, :, zl]
         return remote(block, block, s_s1.at[p, i - 1], r_s1.at[p], target)
 
     def s1(p):
-        arrive(acts.at[p, 0, 0, 0, :, 0], r_s0.at[p])
+        arrive(acts[p].at[0, 0, 0, :, 0], r_s0.at[p])
 
         @pl.when(k == 0)
         def _():
@@ -127,11 +149,11 @@
         if core == 0:
             zz = lax.rem(z + step, 4)
             ys = pl.ds(0, 4) if half is None else pl.ds(half * 2, 2)
-            return acts.at[p, 0, zz // 2, ys, :, lax.rem(zz, 2)]
+            return acts[p].at[0, zz // 2, ys, :, lax.rem(zz, 2)]
         yy = lax.rem(y + step, 4)
         if half is None:
-            return acts.at[p, 1, :, yy]
-        return acts.at[p, 1, half, yy]
+            return acts[p].at[1, :, yy]
+        return acts[p].at[1, half, yy]
 
     def nxt(core, step):
         return at_z(step) if core == 0 else at_y(step)
@@ -155,11 +177,11 @@
         def _():
             f(1)
 
-    full = lambda p: acts.at[p, 0, 0, :, :, 0]
-    half = lambda p: acts.at[p, 0, 0, pl.ds(0, 2), :, 0]
+    full = lambda p: acts[p].at[0, 0, :, :, 0]
+    half = lambda p: acts[p].at[0, 0, pl.ds(0, 2), :, 0]
 
     def s2(p):
-        arrive(acts.at[p, 0, 0, pl.ds(0, 3), :, 0], r_s1.at[p])
+        arrive(acts[p].at[0, 0, pl.ds(0, 3), :, 0], r_s1.at[p])
 
         def go(core):
             s2_copy(p, core, 0).start()
@@ -191,7 +213,7 @@
         by_core(lambda core: s3_copy(p, core, 4).start())
 
     def act_ready(p):
-        arrive(acts.at[p, 0], r_s3.at[p])
+        arrive(acts[p].at[0], r_s3.at[p])
 
     def act_done(p):
         s0_done(p)
@@ -269,39 +291,22 @@
             ring_copy(q, w).wait_send()
         return 0
 
-    seed = jnp.where(k == 0, seed_ref[0], seed_ref[1])
-    row_base = (y * 4 + z) * ROWS
-    col_base = x * COLS
-
-    def hash_chunk(q):
-        it = lax.broadcasted_iota(jnp.int32, (8, COLS), 0)
-        jt = lax.broadcasted_iota(jnp.int32, (8, COLS), 1)
-        base = ((row_base + lsr(it, 2)) * D + col_base + jt) * 4 + (it & 3)
-
-        def two_rows(t, _):
-            for u in range(2):
-                tt = q * (CH // 2) + t * 2 + u
-                h = hash_mix(hash_mix(base + tt * (2 * D * 4)) + seed)
-                words[tt] = jnp.concatenate([h, lsr(h, 16)], 0).astype(jnp.int16)
-            return 0
-
-        lax.fori_loop(0, CH // 4, two_rows, 0)
-
     pair_of = lsr(lax.broadcasted_iota(jnp.int32, (256, 256), 1) & 15, 1)
 
-    def work(q, p_lo, p_hi):
+    def work(q, p_lo, p_hi, between=lambda: None):
         def eight_docs(d, _):
             for c in range(2):
                 for yy in range(4):
                     gt = grads[q, d, c, yy].reshape(SEQ, CH).T
                     for p in range(p_lo, p_hi):
-                        a = acts[p, d, c, yy].reshape(SEQ, PW)
+                        a = acts[p][d, c, yy].reshape(SEQ, PIECE[p])
                         g = jnp.dot(gt, a, preferred_element_type=jnp.float32)
-                        gs[d * 8 + c * 4 + yy, :, p * PW:(p + 1) * PW] = g.astype(BF16)
+                        gs[d * 8 + c * 4 + yy, :, BEGIN[p]:BEGIN[p] + PIECE[p]] = g.astype(BF16)
             return 0
 
         lax.fori_loop(0, 2, eight_docs, 0)
-        lo, hi = p_lo * PW, p_hi * PW
+        between()
+        lo, hi = BEGIN[p_lo], BEGIN[p_hi - 1] + PIECE[p_hi - 1]
 
         def rows_32(t, _):
             for v in range(2):
@@ -330,42 +335,75 @@
     s0(0)
     a2a(0)
     s0(1)
+    s0(2)
+    hash_chunk(2)
     s1(0)
-    s1(1)
-    a2a(1)
-    hash_chunk(0)
+    hash_chunk(3)
     s2(0)
     ring(0)
+    a2a(1)
+    s1(1)
+    hash_chunk(4)
+    s2_on(0)
     s2(1)
-    hash_chunk(1)
-    hash_chunk(2)
-    s2_on(0)
+    ring_on(0)
+    hash_chunk(5)
+    s3(0)
     ring(1)
-    hash_chunk(3)
-    s3(0)
-    ring_on(0)
-    s2_on(1)
+    s1(2)
     a2a(2)
-    hash_chunk(4)
-    a2a(3)
-    s3(1)
+    hash_chunk(6)
     act_ready(0)
     grad_ready(0)
+    work(0, 0, 1, lambda: s2_on(1))
+    s2(2)
+    s3(1)
     ring_on(1)
-    work(0, 0, 1)
-    a2a(4)
-    ring(2)
-    grad_ready(1)
-    work(1, 0, 1)
     act_ready(1)
-    a2a(5)
-    a2a(6)
-    work(0, 1, 2)
-    ring_on(2)
-    ring(3)
-    work(1, 1, 2)
-    hash_chunk(5)
-    hash_chunk(6)
+    work(0, 1, 2, lambda: ring(2))
+    a2a(3)
+
+    def low(q, _):
+        grad_ready(q)
+
+        def between():
+            @pl.when(q == 1)
+            def _():
+                s2_on(2)
+                ring_on(2)
+
+            @pl.when(q == 2)
+            def _():
+                ring(3)
+                a2a(4)
+
+        work(q, 0, 2, between)
+
+        @pl.when(q == 1)
+        def _():
+            s3(2)
+
+        return 0
+
+    lax.fori_loop(1, 3, low, 0)
+    act_ready(2)
+
+    def high(q, _):
+        def between():
+            @pl.when(q == 1)
+            def _():
+                ring_on(3)
+                ring(4)
+
+        work(q, 2, 3, between)
+
+        @pl.when(q < 2)
+        def _():
+            a2a(q + 5)
+
+        return 0
+
+    lax.fori_loop(0, 3, high, 0)
 
     def chunk(q, _):
         grad_ready(q)
@@ -378,10 +416,10 @@
         def _():
             ring(q + 2)
 
-        work(q, 0, 2)
+        work(q, 0, 3)
         return 0
 
-    lax.fori_loop(2, NQ, chunk, 0)
+    lax.fori_loop(3, NQ, chunk, 0)
 
     ri = lax.broadcasted_iota(jnp.int32, (256, 256), 0)
     ci = lax.broadcasted_iota(jnp.int32, (256, 256), 1)
@@ -409,6 +447,9 @@
 
     pltpu.make_async_copy(part.at[row], fin1.at[row], r_f1).start()
     lax.fori_loop(1, 16, lambda j, _: (f1_copy(j).start(), 0)[1], 0)
+    for p in range(NP):
+        act_done(p)
+    lax.fori_loop(0, NQ, grad_done, 0)
     arrive(fin1, r_f1)
     for m in range(2):
         total = fin1[m]
@@ -428,9 +469,6 @@
         total = total + fin2[c]
     out_ref[...] = total * (1.0 / math.sqrt(SEQ * D * FF))
 
-    for p in range(NP):
-        act_done(p)
-    lax.fori_loop(0, NQ, grad_done, 0)
     sent = part.at[pl.ds(0, 15)]
     pltpu.make_async_copy(sent, sent, s_f1).wait()
     for j in range(1, 8):
@@ -445,7 +483,7 @@
         in_specs=[pl.BlockSpec(memory_space=pl.ANY)] * 3 + [pl.BlockSpec(memory_space=pltpu.SMEM)] * 2,
         out_specs=pl.BlockSpec(memory_space=pltpu.VMEM),
         scratch_shapes=[
-            pltpu.VMEM((NP, 2, 2, 4, 4, 2, 32, PW), BF16),
+            *[pltpu.VMEM((2, 2, 4, 4, 2, 32, width), BF16) for width in PIECE],
             pltpu.VMEM((NQ, 2, 2, 4, 4, 2, 32, CH), BF16),
             pltpu.VMEM((ROWS // 2, 16, COLS), jnp.int16),
             pltpu.VMEM((16, CH, COLS), BF16),

time: 147 us -> 143 us (0.973)
  Pallas kernels: 146 us -> 141 us
    pallas_call x1, Pallas kernels: 146 us -> 141 us  [shards(): pl.pallas_call(kernel, out_shape=jax.ShapeDtypeStruct((2, 8, K), jnp.floa...]
where the time goes in v2:
time: 143 us
  Pallas kernels  141 us (99%)
    pallas_call x1, Pallas kernels, shards(): pl.pallas_call(kernel, out_shape=jax.ShapeDtypeStruct((2, 8, K), jnp.floa...  141 us

profile of v2, /device:TPU:1, one launch (start us, length us, event | category | flops | bytes accessed | tf_op | source)
XLA Modules:
  0.0 142.6 jit_solution(9957830707206242676)
XLA Ops:
  0.0 141.3 %sketch.1 = f32[2,8,128]{2,1,0:T(8,128)} custom-call(bf16[32,4096]{1,0:T(8,128)(2,1)} %act_in.1, bf16[32,14336]{1,0:T(8,128)(2,1)} %gate_in.1, bf16[32,14336]{1,0:T(8,128)(2,1)} %up_in.1, s32[16]{0:T(128)} %order_ref.1, s32[2]{0:T(128)} %seed_ref.1), custom_call_target="tpu_custom_call" | custom-call | tf_op jit(solution)/shard_map/sketch/pallas_call | solution.py:480
  141.3 1.3 constant_dynamic-slice_fusion

commit v3 on v2

--- a/solution.py
+++ b/solution.py
@@ -304,17 +304,18 @@
                         gs[d * 8 + c * 4 + yy, :, BEGIN[p]:BEGIN[p] + PIECE[p]] = g.astype(BF16)
             return 0
 
-        lax.fori_loop(0, 2, eight_docs, 0)
+        eight_docs(0, 0)
+        eight_docs(1, 0)
         between()
         lo, hi = BEGIN[p_lo], BEGIN[p_hi - 1] + PIECE[p_hi - 1]
 
-        def rows_32(t, _):
-            for v in range(2):
-                begin = pl.multiple_of(t * 32 + v * 16, 16)
+        def rows_64(t, _):
+            for v in range(4):
+                begin = pl.multiple_of(t * 64 + v * 16, 16)
                 g = jnp.concatenate([gs[n, pl.ds(begin, 16), lo:hi] for n in range(16)], 0)
                 picked = None
                 for pair in range(8):
-                    w = words[q * (CH // 2) + t * 16 + v * 8 + pair, :, lo:hi]
+                    w = words[q * (CH // 2) + t * 32 + v * 8 + pair, :, lo:hi]
                     s = jnp.concatenate(
                         [
                             jnp.where(
@@ -329,7 +330,7 @@
                 acc[...] += picked
             return 0
 
-        lax.fori_loop(0, CH // 32, rows_32, 0)
+        lax.fori_loop(0, CH // 64, rows_64, 0)
 
     acc[...] = jnp.zeros_like(acc)
     s0(0)
@@ -352,7 +353,6 @@
     ring(1)
     s1(2)
     a2a(2)
-    hash_chunk(6)
     act_ready(0)
     grad_ready(0)
     work(0, 0, 1, lambda: s2_on(1))
@@ -370,6 +370,7 @@
             @pl.when(q == 1)
             def _():
                 s2_on(2)
+                hash_chunk(6)
                 ring_on(2)
 
             @pl.when(q == 2)

time: 143 us -> 139 us (0.972)
  Pallas kernels: 141 us -> 137 us
    pallas_call x1, Pallas kernels: 141 us -> 137 us  [shards(): pl.pallas_call(kernel, out_shape=jax.ShapeDtypeStruct((2, 8, K), jnp.floa...]
where the time goes in v3:
time: 139 us
  Pallas kernels  137 us (99%)
    pallas_call x1, Pallas kernels, shards(): pl.pallas_call(kernel, out_shape=jax.ShapeDtypeStruct((2, 8, K), jnp.floa...  137 us

profile of v3, /device:TPU:1, one launch (start us, length us, event | category | flops | bytes accessed | tf_op | source)
XLA Modules:
  0.0 138.8 jit_solution(11027577908390826328)
XLA Ops:
  0.0 137.5 %sketch.1 = f32[2,8,128]{2,1,0:T(8,128)} custom-call(bf16[32,4096]{1,0:T(8,128)(2,1)} %act_in.1, bf16[32,14336]{1,0:T(8,128)(2,1)} %gate_in.1, bf16[32,14336]{1,0:T(8,128)(2,1)} %up_in.1, s32[16]{0:T(128)} %order_ref.1, s32[2]{0:T(128)} %seed_ref.1), custom_call_target="tpu_custom_call" | custom-call | tf_op jit(solution)/shard_map/sketch/pallas_call | solution.py:481
  137.5 1.3 constant_dynamic-slice_fusion

commit v4 on v3

--- a/solution.py
+++ b/solution.py
@@ -117,7 +117,7 @@
         return lambda p: act_in.at[:, pl.ds(pl.multiple_of(c * COLS + BEGIN[p], 256), PIECE[p])]
 
     def s0(p):
-        own = acts[p].at[k, zh, y, x, zl]
+        own = acts[p].at[k, zh, zl, y, x]
         pltpu.make_async_copy(act_slice(x)(p), own, r_s0.at[p]).start()
         for dx in range(1, 4):
             c = lax.rem(x + dx, 4)
@@ -125,15 +125,15 @@
 
     def s0_done(p):
         for dx in range(1, 4):
-            own = acts[p].at[k, zh, y, x, zl]
+            own = acts[p].at[k, zh, zl, y, x]
             remote(act_slice(lax.rem(x + dx, 4))(p), own, s_s0.at[p, dx - 1], r_s0.at[p], at_x(dx)).wait_send()
 
     def s1_copy(p, i, target):
-        block = acts[p].at[k, zh, y, :, zl]
+        block = acts[p].at[k, zh, zl, y]
         return remote(block, block, s_s1.at[p, i - 1], r_s1.at[p], target)
 
     def s1(p):
-        arrive(acts[p].at[0, 0, 0, :, 0], r_s0.at[p])
+        arrive(acts[p].at[0, 0, 0, 0], r_s0.at[p])
 
         @pl.when(k == 0)
         def _():
@@ -149,11 +149,11 @@
         if core == 0:
             zz = lax.rem(z + step, 4)
             ys = pl.ds(0, 4) if half is None else pl.ds(half * 2, 2)
-            return acts[p].at[0, zz // 2, ys, :, lax.rem(zz, 2)]
+            return acts[p].at[0, zz // 2, lax.rem(zz, 2), ys]
         yy = lax.rem(y + step, 4)
         if half is None:
-            return acts[p].at[1, :, yy]
-        return acts[p].at[1, half, yy]
+            return acts[p].at[1, :, :, yy]
+        return acts[p].at[1, half, :, yy]
 
     def nxt(core, step):
         return at_z(step) if core == 0 else at_y(step)
@@ -177,11 +177,11 @@
         def _():
             f(1)
 
-    full = lambda p: acts[p].at[0, 0, :, :, 0]
-    half = lambda p: acts[p].at[0, 0, pl.ds(0, 2), :, 0]
+    full = lambda p: acts[p].at[0, 0, 0]
+    half = lambda p: acts[p].at[0, 0, 0, pl.ds(0, 2)]
 
     def s2(p):
-        arrive(acts[p].at[0, 0, pl.ds(0, 3), :, 0], r_s1.at[p])
+        arrive(acts[p].at[0, 0, 0, pl.ds(0, 3)], r_s1.at[p])
 
         def go(core):
             s2_copy(p, core, 0).start()
@@ -297,9 +297,9 @@
         def eight_docs(d, _):
             for c in range(2):
                 for yy in range(4):
-                    gt = grads[q, d, c, yy].reshape(SEQ, CH).T
+                    gt = jnp.concatenate([grads[q, d, c, yy, i % 4, i // 4] for i in range(8)], 0).T
                     for p in range(p_lo, p_hi):
-                        a = acts[p][d, c, yy].reshape(SEQ, PIECE[p])
+                        a = acts[p][d, c, :, yy].reshape(SEQ, PIECE[p])
                         g = jnp.dot(gt, a, preferred_element_type=jnp.float32)
                         gs[d * 8 + c * 4 + yy, :, BEGIN[p]:BEGIN[p] + PIECE[p]] = g.astype(BF16)
             return 0
@@ -308,14 +308,15 @@
         eight_docs(1, 0)
         between()
         lo, hi = BEGIN[p_lo], BEGIN[p_hi - 1] + PIECE[p_hi - 1]
-
-        def rows_64(t, _):
-            for v in range(4):
-                begin = pl.multiple_of(t * 64 + v * 16, 16)
+        step = 64 if hi - lo == COLS else CH
+
+        def some_rows(t, _):
+            for v in range(step // 16):
+                begin = pl.multiple_of(t * step + v * 16, 16)
                 g = jnp.concatenate([gs[n, pl.ds(begin, 16), lo:hi] for n in range(16)], 0)
                 picked = None
                 for pair in range(8):
-                    w = words[q * (CH // 2) + t * 32 + v * 8 + pair, :, lo:hi]
+                    w = words[q * (CH // 2) + t * (step // 2) + v * 8 + pair, :, lo:hi]
                     s = jnp.concatenate(
                         [
                             jnp.where(
@@ -330,7 +331,7 @@
                 acc[...] += picked
             return 0
 
-        lax.fori_loop(0, CH // 64, rows_64, 0)
+        lax.fori_loop(0, CH // step, some_rows, 0)
 
     acc[...] = jnp.zeros_like(acc)
     s0(0)
@@ -484,7 +485,7 @@
         in_specs=[pl.BlockSpec(memory_space=pl.ANY)] * 3 + [pl.BlockSpec(memory_space=pltpu.SMEM)] * 2,
         out_specs=pl.BlockSpec(memory_space=pltpu.VMEM),
         scratch_shapes=[
-            *[pltpu.VMEM((2, 2, 4, 4, 2, 32, width), BF16) for width in PIECE],
+            *[pltpu.VMEM((2, 2, 2, 4, 4, 32, width), BF16) for width in PIECE],
             pltpu.VMEM((NQ, 2, 2, 4, 4, 2, 32, CH), BF16),
             pltpu.VMEM((ROWS // 2, 16, COLS), jnp.int16),
             pltpu.VMEM((16, CH, COLS), BF16),

time: 139 us -> 138 us (level)
  no operation moved by 1% of the time
where the time goes in v4:
time: 138 us
  Pallas kernels  137 us (99%)
    pallas_call x1, Pallas kernels, shards(): pl.pallas_call(kernel, out_shape=jax.ShapeDtypeStruct((2, 8, K), jnp.floa...  137 us

profile of v4, /device:TPU:1, one launch (start us, length us, event | category | flops | bytes accessed | tf_op | source)
XLA Modules:
  0.0 137.9 jit_solution(1714820058374595107)
XLA Ops:
  0.0 136.6 %sketch.1 = f32[2,8,128]{2,1,0:T(8,128)} custom-call(bf16[32,4096]{1,0:T(8,128)(2,1)} %act_in.1, bf16[32,14336]{1,0:T(8,128)(2,1)} %gate_in.1, bf16[32,14336]{1,0:T(8,128)(2,1)} %up_in.1, s32[16]{0:T(128)} %order_ref.1, s32[2]{0:T(128)} %seed_ref.1), custom_call_target="tpu_custom_call" | custom-call | tf_op jit(solution)/shard_map/sketch/pallas_call | solution.py:482
  136.6 1.3 constant_dynamic-slice_fusion
